TPU v7x, 256 devices: a whole 4x4x8 slice. The times are simulated.
256 devices in a mesh: rows: 32 (over x, z), cols: 8 (over y, core).
Axes of the slice: x: 4, y: 4, z: 8, core: 2. Of those that a mesh axis runs over, the one named last changes fastest.
Arguments:
- weight: bfloat16 [8192, 28672], P('cols', 'rows'), may hold values from -0.6 to 0.6
- calib: bfloat16 [2048, 8192], P('rows', 'cols'), may hold values from -180 to 180
- sketch: bfloat16 [28672, 256], P('rows'), may hold values from -6 to 6
Outputs:
- sparse: bfloat16 [8192, 28672], P('cols', 'rows')
- basis: bfloat16 [8192, 256], P('cols')
- coeffs: bfloat16 [256, 28672], P(None, 'rows')
- out_error: float32 [2048, 28672], P('cols', 'rows')
All inputs are finite; a program needn't handle non-finite values.
Results may differ from a plain program's by a relative error of at most 0.023.
Values may be sent and summed in bfloat16 or wider, within the bound.
A program may use at most 64 MiB of HBM per device.

v0:
```python
import jax
import jax.numpy as jnp
from jax import lax
from jax.sharding import PartitionSpec as P


def orthonormal(gram, ranged):
    chol = jnp.linalg.cholesky(gram)
    return jax.scipy.linalg.solve_triangular(chol, ranged.T, lower=True).T.astype(jnp.bfloat16)


def shards(weight, calib, sketch):
    xval = calib.astype(jnp.float32)
    energy = lax.psum(jnp.sum(xval * xval, axis=0), "rows")
    tokens_all = calib.shape[0] * lax.axis_size("rows")
    scale = jnp.sqrt(energy / tokens_all + 1e-06)
    scaled = scale[:, None] * weight.astype(jnp.float32)
    total = lax.psum(jnp.sum(jnp.abs(scaled)), ("rows", "cols"))
    entries = weight.shape[0] * lax.axis_size("cols") * weight.shape[1] * lax.axis_size("rows")
    tau = 2.0 * total / entries
    clipped = jnp.clip(scaled, -tau, tau)
    sparse = (scaled - clipped).astype(jnp.bfloat16)
    resid = clipped.astype(jnp.bfloat16)
    xs = (xval / scale[None, :]).astype(jnp.bfloat16)
    whole_x = lax.all_gather(xs, "rows", axis=0, tiled=True)
    partial_value = jnp.dot(resid, sketch, preferred_element_type=jnp.float32)
    ranged = lax.psum(partial_value, "rows")
    gram = lax.psum(jnp.dot(ranged.T, ranged, precision=lax.Precision.HIGHEST), "cols")
    basis = orthonormal(gram, ranged)
    term = lax.dot_general(
        basis, resid, (((0,), (0,)), ((), ())), preferred_element_type=jnp.float32
    )
    coeffs = lax.psum(term, "cols").astype(jnp.bfloat16)
    err = (
        resid.astype(jnp.float32) - jnp.dot(basis, coeffs, preferred_element_type=jnp.float32)
    ).astype(jnp.bfloat16)
    out_error = lax.psum_scatter(
        jnp.dot(whole_x, err, preferred_element_type=jnp.float32).astype(jnp.bfloat16),
        "cols",
        scatter_dimension=0,
        tiled=True,
    ).astype(jnp.float32)
    return (sparse, basis, coeffs, out_error)


def solution(mesh):
    return jax.shard_map(
        shards,
        mesh=mesh,
        in_specs=(P("cols", "rows"), P("rows", "cols"), P("rows", None)),
        out_specs=(P("cols", "rows"), P("cols", None), P(None, "rows"), P("cols", "rows")),
        check_vma=False,
    )
```

profile of v0, /device:TPU:1, one launch (start us, length us, event | category | flops | bytes accessed | tf_op | source)
XLA Modules:
  0.0 541.0 jit_solution(1585133642807060905)
XLA Ops:
  8.2 64.4 %psum.35 = f32[1024]{0:T(1024)S(1)} all-reduce(f32[1024]{0:T(1024)S(1)} %fusion.3), channel_id=1, replica_groups=mesh['rows'=32,'cols'=8] {'rows'}, use_global_device_ids=true, to_apply=%region_1.0 | all-reduce | flops 1024 | bytes 8192 | tf_op jit(solution)/shard_map/psum | solution.py:14
  72.6 3.3 abs_reduce_fusion
  75.9 88.1 %psum.36 = f32[]{:T(128)} all-reduce(f32[]{:T(128)} %abs_reduce_fusion), channel_id=1, replica_groups=mesh['rows'=32,'cols'=8] {'rows','cols'}, use_global_device_ids=true, to_apply=%region_3.0 | all-reduce | flops 1 | bytes 8 | tf_op jit(solution)/shard_map/psum | solution.py:18
  164.6 3.3 fusion.17
  168.0 139.5 %all-reduce.5.cloned.1.call-done = f32[1024,256]{1,0:T(8,128)} async-done(((f32[1024,256]{1,0:T(8,128)}), f32[1024,256]{1,0:T(8,128)}) %all-reduce.5.cloned.1.call-update) | async-done | bytes 1048592 | tf_op jit(solution)/shard_map/psum | solution.py:27
  307.5 4.1 fusion.21
  312.7 64.1 %all-reduce.7.cloned.1.call-done = f32[256,256]{0,1:T(8,128)} async-done(((f32[256,256]{0,1:T(8,128)}), f32[256,256]{0,1:T(8,128)}) %all-reduce.7.cloned.1.call-update) | async-done | bytes 262160 | tf_op jit(solution)/shard_map/psum | solution.py:28
  376.8 1.8 copy.8
  380.5 11.7 %cholesky.50 = f32[128,128]{1,0:T(8,128)S(1)} custom-call(f32[128,128]{1,0:T(8,128)S(1)} %cholesky.118), custom_call_target="Cholesky" | custom-call | tf_op jit(solution)/shard_map/jit(cholesky)/cholesky | solution.py:8
  392.2 9.8 %custom-call.15 = f32[1,128,128]{1,2,0:T(8,128)S(1)} custom-call(f32[1,128,128]{2,1,0:T(8,128)S(1)} %get-tuple-element.29), custom_call_target="InvertDiagBlocksLowerTriangular" | custom-call | tf_op jit(solution)/shard_map/jit(cholesky)/cholesky | solution.py:8
  402.8 1.7 constant_dynamic-update-slice_fusion.1
  405.5 11.7 %cholesky.105 = f32[128,128]{1,0:T(8,128)S(1)} custom-call(f32[128,128]{1,0:T(8,128)S(1)} %convolution_subtract_fusion.1), custom_call_target="Cholesky" | custom-call | tf_op jit(solution)/shard_map/jit(cholesky)/cholesky | solution.py:8
  419.8 1.7 select_select_fusion
  421.6 6.9 %while.1 = (s32[]{:T(128)}, f32[256,256]{1,0:T(8,128)}, s32[2,2]{1,0:T(2,128)S(1)}, f32[2,128,128]{2,1,0:T(8,128)}, s32[]{:T(128)}) while((s32[]{:T(128)}, f32[256,256]{1,0:T(8,128)}, s32[2,2]{1,0:T(2,128)S(1)}, f32[2,128,128]{2,1,0:T(8,128)}, s32[]{:T(128)}) %tuple.29), condition=%wide.while_cond, body=%wide.while_body.sunk | while | flops 2 | bytes 132705 | solution.py:9
  422.2 2.9 bitcast_dynamic-update-slice_fusion.2
  425.7 2.8 bitcast_dynamic-update-slice_fusion.2
  428.6 20.5 %custom-call.16 = f32[2,128,128]{1,2,0:T(8,128)S(1)} custom-call(f32[2,128,128]{2,1,0:T(8,128)} %get-tuple-element.11), custom_call_target="InvertDiagBlocksLowerTriangular" | custom-call | tf_op jit(solution)/shard_map/jit(_solve_triangular)/triangular_solve | solution.py:9
  449.7 1.9 convolution_subtract_fusion
  452.3 1.8 fusion.6
  454.1 31.0 %all-reduce.8 = bf16[256,896]{1,0:T(8,128)(2,1)S(1)} all-reduce(f32[256,896]{1,0:T(8,128)} %fusion.6), channel_id=1, replica_groups=mesh['rows'=32,'cols'=8] {'cols'}, use_global_device_ids=true, to_apply=%region_10.11 | all-reduce | flops 229376 | bytes 1376256 | tf_op jit(solution)/shard_map/psum | solution.py:33
  485.2 8.9 %convolution_convert_fusion = bf16[2048,896]{1,0:T(8,128)(2,1)} fusion(bf16[2048,1024]{1,0:T(8,128)(2,1)} %all-gather.2.cloned.1.call-done, bf16[256,896]{1,0:T(8,128)(2,1)S(1)} %all-reduce.8, bf16[128,1024]{1,0:T(8,128)(2,1)S(1)} %convolution_convert_fusion.1, bf16[128,1024]{1,0:T(8,128)(2,1)} %copy-done.3, bf16[1024,896]{1,0:T(8,128)(2,1)S(1)} %copy-done.2, ...), kind=kOutput, calls=%fused_computation.8 | convolution fusion | flops 4238999552 | bytes 10686472 | tf_op jit(solution)/shard_map/dot_general | solution.py:38
  494.1 2.0 subtract_convert_fusion.1
  497.1 35.4 %reduce-scatter.2.cloned.1.call-done = bf16[256,896]{1,0:T(8,128)(2,1)} async-done(((bf16[2048,896]{1,0:T(8,128)(2,1)}), bf16[256,896]{1,0:T(8,128)(2,1)}) %reduce-scatter.2.cloned.1.call-update) | async-done | bytes 458768 | tf_op jit(solution)/shard_map/reduce_scatter | solution.py:37
  532.5 2.0 convert_element_type.44
  (46 shorter events, 10.8 us)
Async XLA Ops:
  7.2 157.4 %copy-start = (bf16[896,256]{1,0:T(8,128)(2,1)S(1)}, bf16[896,256]{1,0:T(8,128)(2,1)}, u32[]{:S(2)}) copy-start(bf16[896,256]{1,0:T(8,128)(2,1)} %param.5) | copy-start | bytes 1376260
  7.2 300.3 %all-reduce.5.cloned.1.call-start = ((), (), s32[]{:S(2)}) async-start(), calls=%async_computation.1 | async-start | bytes 2097152 | tf_op jit(solution)/shard_map/psum | solution.py:27
  164.6 147.1 %copy-start.6 = (bf16[64,1024]{1,0:T(8,128)(2,1)S(1)}, bf16[64,1024]{1,0:T(8,128)(2,1)}, u32[]{:S(2)}) copy-start(bf16[64,1024]{1,0:T(8,128)(2,1)} %param.4) | copy-start | bytes 393220
  167.9 208.8 %all-reduce.7.cloned.1.call-start = ((), (), s32[]{:S(2)}) async-start(), calls=%async_computation.2 | async-start | bytes 524288 | tf_op jit(solution)/shard_map/psum | solution.py:28
  307.5 141.5 %copy-start.1 = (f32[1024,256]{1,0:T(8,128)S(1)}, f32[1024,256]{1,0:T(8,128)}, u32[]{:S(2)}) copy-start(f32[1024,256]{1,0:T(8,128)} %all-reduce.5.cloned.1.call-done) | copy-start | bytes 3145732
  311.7 173.5 %all-gather.2.cloned.1.call-start = ((), (), s32[]{:S(2)}) async-start(), calls=%async_computation.3 | async-start | bytes 4325376 | tf_op jit(solution)/shard_map/all_gather | solution.py:25
  312.5 220.0 %reduce-scatter.2.cloned.1.call-start = ((), (), s32[]{:S(2)}) async-start(), calls=%async_computation.4 | async-start | bytes 4128768 | tf_op jit(solution)/shard_map/reduce_scatter | solution.py:37
  378.6 73.7 %copy-start.2 = (bf16[1024,896]{1,0:T(8,128)(2,1)S(1)}, bf16[1024,896]{1,0:T(8,128)(2,1)}, u32[]{:S(2)}) copy-start(bf16[1024,896]{1,0:T(8,128)(2,1)} %param.3) | copy-start | bytes 5505028
  379.8 0.7 copy-start.5
  449.7 2.6 copy-start.3
  485.1 9.0 %copy-start.7 = (bf16[256,896]{1,0:T(8,128)(2,1)}, bf16[256,896]{1,0:T(8,128)(2,1)S(1)}, u32[]{:S(2)}) copy-start(bf16[256,896]{1,0:T(8,128)(2,1)S(1)} %all-reduce.8) | copy-start | bytes 1376260
  494.1 2.0 copy-start.4
Sparse Core Ops, SparseCore 0:
  168.1 139.3 all-reduce.4
  311.8 64.9 all-reduce.6
  380.3 80.6 all-gather.1
  494.2 38.1 reduce-scatter.1
where the time goes:
time: 544 us; the launch traced here: 541 us
  waiting for transfers between devices  239 us (44%)
  blocking collectives  183 us (34%)
  other arithmetic  66.9 us (12%)
  matrix products  24.2 us (4%)
  between operations  15.9 us (3%)
  local copies, waits for them, and re-layouts  11.3 us (2%)
    psum x1, waiting for transfers between devices, shards(): ranged = lax.psum(partial_value, 'rows')  140 us
    psum x1, blocking collectives, shards(): total = lax.psum(jnp.sum(jnp.abs(scaled)), ('rows', 'cols'))  88.1 us
    psum x1, blocking collectives, shards(): energy = lax.psum(jnp.sum(xval * xval, axis=0), 'rows')  64.4 us
    psum x1, waiting for transfers between devices, shards(): lax.psum(jnp.dot(ranged.T, ranged, precision=lax.Precision.HIGHEST), 'cols')  64.1 us
    reduce_scatter x1, waiting for transfers between devices, shards(): lax.psum_scatter(jnp.dot(whole_x, err, preferred_element_type=jnp.float32...  35.4 us
    another operation x6, other arithmetic, orthonormal(): chol = jnp.linalg.cholesky(gram)  34.6 us
    psum x1, blocking collectives, shards(): coeffs = lax.psum(term, 'cols').astype(jnp.bfloat16)  31 us
    another operation x3, other arithmetic, orthonormal(): jax.scipy.linalg.solve_triangular(chol, ranged.T, lower=True)  22.2 us
  transfers between devices with their start and end apart: 4, of which 3 were waited for; matrix products, arithmetic and copies ran while one was open for 15% of the time, Pallas kernels for 0%

commit v1 on v0

v1 whole, which is shorter than its diff:
```python
import jax
import jax.numpy as jnp
from jax import lax
from jax.experimental import pallas as pl
from jax.experimental.pallas import tpu as pltpu
from jax.sharding import PartitionSpec as P

MESH = pl.DeviceIdType.MESH
F32, BF16 = jnp.float32, jnp.bfloat16
NX, NZ, NY = 4, 8, 4
RANK = 256
PANEL = 32


def split3(v):
    a = v.astype(BF16)
    rest = v - a.astype(F32)
    b = rest.astype(BF16)
    return a, b, (rest - b.astype(F32)).astype(BF16)


def split2(v):
    a = v.astype(BF16)
    return a, (v - a.astype(F32)).astype(BF16)


def dot(a, b, ca, cb):
    return lax.dot_general(a, b, (((ca,), (cb,)), ((), ())), preferred_element_type=F32)


def inverse_factor(m_ref, out_ref):
    lane = lax.broadcasted_iota(jnp.int32, (PANEL, 2 * RANK), 1)
    sub8 = lax.broadcasted_iota(jnp.int32, (8, 128), 0)
    groups = PANEL // 8

    def panel(step, carry):
        k0 = pl.multiple_of(step * PANEL, PANEL)
        rows = m_ref[pl.ds(k0, PANEL), :]
        rows = jnp.where(lane >= k0, rows, 0.0)
        diag = pltpu.roll(rows[:, :RANK], lax.rem(RANK - k0, RANK), 1)[:, :128]
        rg = [rows[8 * g:8 * g + 8, :] for g in range(groups)]
        dg = [diag[8 * g:8 * g + 8, :] for g in range(groups)]
        for q in range(groups):
            left = range(groups - q)
            col = [
                [jnp.broadcast_to(dg[g][:, 8 * q + j:8 * q + j + 1], (8, 128)) for g in range(q, groups)]
                for j in range(8)
            ]
            pivots = jnp.zeros((8, 128), F32)
            for j in range(8):
                pivot = jnp.broadcast_to(col[j][0][j:j + 1, :], (8, 128))
                inv = 1.0 / pivot
                pivots = jnp.where(sub8 == j, pivot, pivots)
                mult = [col[j][g] * inv for g in left]
                mult[0] = jnp.where(sub8 > j, mult[0], 0.0)
                for other in range(j + 1, 8):
                    row = jnp.broadcast_to(col[other][0][j:j + 1, :], (8, 128))
                    for g in left:
                        col[other][g] = col[other][g] - mult[g] * row
                rrow, drow = rg[q][j:j + 1, :], dg[q][j:j + 1, :]
                for g in left:
                    rg[q + g] = rg[q + g] - jnp.concatenate([mult[g]] * 4, axis=1) * rrow
                    dg[q + g] = dg[q + g] - mult[g] * drow
            root = lax.rsqrt(pivots)
            rg[q] = rg[q] * jnp.concatenate([root] * 4, axis=1)
        done = jnp.concatenate(rg, axis=0)
        out_ref[pl.ds(k0, PANEL), :] = done[:, RANK:]
        a, b, c = split3(done)
        lhs = jnp.concatenate([a, a, b, a, b, c], axis=0)[:, :RANK]
        rhs = jnp.concatenate([a, b, a, c, b, a], axis=0)
        m_ref[...] -= dot(lhs, rhs, 0, 0)
        return carry

    lax.fori_loop(0, RANK // PANEL, panel, 0)


def exchange_kernel(
    w_ref, cal_in, sk_ref,
    a_out, q_out, linv_out, rng, z_out, scale_out, tau_out,
    cal, stx, stx_in, stz, stz_in, tsend, t_in, resid, rclip, rp, rx_in, rzs, rz_in,
    gp, gcore, gs, gy_in, gown, gfull, zp, zcore, zs, zy_in, qp, qcore, qs, qy_in, ap, acore, asum, ay_in, m_ref, rscaled,
    ssem, rsem,
):
    rr, cc = lax.axis_index("rows"), lax.axis_index("cols")
    x, z = rr // NZ, lax.rem(rr, NZ)
    y, k = cc // 2, lax.rem(cc, 2)
    sib = 1 - k

    def xat(d):
        return lax.rem(x + d, NX)

    def zat(d):
        return lax.rem(z + d, NZ)

    def yat(d):
        return lax.rem(y + d, NY)

    def dev(xx=x, zz=z, yy=y, kk=k):
        return (xx * NZ + zz, yy * 2 + kk)

    count = [0]
    pending = []

    def send(src, dst, to):
        i = count[0]
        count[0] += 1
        copy = pltpu.make_async_remote_copy(
            src_ref=src, dst_ref=dst, send_sem=ssem.at[i], recv_sem=rsem.at[i], device_id=to, device_id_type=MESH
        )
        copy.start()
        pending.append(copy)
        return copy

    def arrive(copies):
        for copy in copies:
            copy.wait_recv()

    barrier = pltpu.get_barrier_semaphore()
    partners = [dev(xx=xat(d)) for d in range(1, NX)] + [dev(zz=zat(d)) for d in range(1, NZ)]
    partners += [(rr, lax.rem(cc + d, 8)) for d in range(1, 8)]
    for p in partners:
        pl.semaphore_signal(barrier, inc=1, device_id=p, device_id_type=MESH)

    for i in range(2):
        part = cal_in[:, 512 * i:512 * i + 512].astype(F32)
        stx[0:1, 512 * i:512 * i + 512] = jnp.sum(part * part, axis=0, keepdims=True)
    ones = jnp.ones((8, w_ref.shape[1]), BF16)
    for i in range(4):
        stx[1:2, 256 * i:256 * i + 256] = dot(ones, jnp.abs(w_ref[256 * i:256 * i + 256, :]), 1, 1)[0:1, :]
    pl.semaphore_wait(barrier, len(partners))

    sx = [send(stx, stx_in.at[d - 1], dev(xx=xat(d))) for d in range(1, NX)]

    xs_plus, xs_minus, zs_plus, zs_minus = xat(1), xat(NX - 1), zat(1), zat(NZ - 1)
    own = cal.at[x, z]
    own[...] = cal_in[...]

    def h0x1():
        return [send(cal.at[x, z, 0:32], cal.at[x, z, 0:32], dev(xx=xs_plus)),
                send(cal.at[x, z, 0:32], cal.at[x, z, 0:32], dev(xx=xs_minus))]

    def h0x2():
        lo, hi = cal.at[xs_minus, z, 0:16], cal.at[xs_plus, z, 16:32]
        return [send(lo, lo, dev(xx=xs_plus)), send(hi, hi, dev(xx=xs_minus))]

    def h1z(step):
        lo, hi = zat(NZ - step + 1), zat(step - 1)
        tl, th = (slice(32, 64), slice(32, 64)) if step < 4 else (slice(32, 48), slice(48, 64))
        up, down = cal.at[x, lo, tl], cal.at[x, hi, th]
        return [send(up, up, dev(zz=zs_plus)), send(down, down, dev(zz=zs_minus))]

    def h0z(step):
        lo, hi = zat(NZ - step + 1), zat(step - 1)
        tl, th = (slice(0, 32), slice(0, 32)) if step < 4 else (slice(0, 16), slice(16, 32))
        up, down = cal.at[:, lo, tl], cal.at[:, hi, th]
        return [send(up, up, dev(zz=zs_plus)), send(down, down, dev(zz=zs_minus))]

    def h1x1():
        block = cal.at[x, :, 32:64]
        return [send(block, block, dev(xx=xs_plus)), send(block, block, dev(xx=xs_minus))]

    def h1x2():
        lo, hi = cal.at[xs_minus, :, 32:48], cal.at[xs_plus, :, 48:64]
        return [send(lo, lo, dev(xx=xs_plus)), send(hi, hi, dev(xx=xs_minus))]

    g_x, g_z = h0x1(), h1z(1)

    arrive(sx)
    stz[...] = stx[...] + stx_in[0] + stx_in[1] + stx_in[2]
    sz = [send(stz, stz_in.at[d - 1], dev(zz=zat(d))) for d in range(1, NZ)]
    arrive(g_x)
    g_x = h0x2()
    arrive(g_z)
    g_z = h1z(2)
    arrive(sz)
    tot = stz[...]
    for d in range(1, NZ):
        tot = tot + stz_in[d - 1]
    scale_row = jnp.sqrt(tot[0:1, :] / (NX * NZ * cal_in.shape[0]) + 1e-06)
    mine = jnp.sum(scale_row * tot[1:2, :], axis=1, keepdims=True)
    tsend[...] = jnp.broadcast_to(mine, (8, 128))
    st = [send(tsend, t_in.at[d - 1], (rr, lax.rem(cc + d, 8))) for d in range(1, 8)]
    arrive(g_x)
    g_h0z = h0z(1)
    arrive(g_z)
    g_z = h1z(3)
    for i in range(8):
        row = scale_row[:, 128 * i:128 * i + 128]
        scale_out[128 * i:128 * i + 128, :] = jnp.transpose(jnp.broadcast_to(row, (128, 128)))
    arrive(st)
    total = tsend[...]
    for d in range(1, 8):
        total = total + t_in[d - 1]
    tau_out[...] = total * (2.0 / (float(w_ref.shape[0] * 8) * float(w_ref.shape[1] * NX * NZ)))
    tau = tau_out[0:1, 0:1]

    def clip_rows(i, carry):
        sl = pl.ds(pl.multiple_of(i * 32, 32), 32)
        sc = scale_out[sl, 0:1]
        lim = tau / sc
        w = w_ref[sl, :].astype(F32)
        resid[sl, :] = jnp.clip(sc * w, -tau, tau).astype(BF16)
        rclip[sl, :] = jnp.clip(w, -lim, lim).astype(BF16)
        return carry

    lax.fori_loop(0, w_ref.shape[0] // 32, clip_rows, 0)
    arrive(g_z)
    g_z = h1z(4)
    arrive(g_h0z)
    g_h0z = h0z(2)

    nrow = w_ref.shape[0] // NX
    for i in range(NX):
        rp[i] = dot(resid[i * nrow:(i + 1) * nrow, :], sk_ref[...], 1, 0).astype(BF16)
    sx = [send(rp.at[xat(d)], rx_in.at[d - 1], dev(xx=xat(d))) for d in range(1, NX)]
    arrive(g_z)
    g_h1x = h1x1()
    arrive(sx)
    part = rp[x].astype(F32)
    for d in range(1, NX):
        part = part + rx_in[d - 1].astype(F32)
    rzs[...] = part.astype(BF16).reshape(NZ, nrow // NZ, RANK)
    sz = [send(rzs.at[zat(d)], rz_in.at[d - 1], dev(zz=zat(d))) for d in range(1, NZ)]
    arrive(g_h0z)
    g_h0z = h0z(3)
    arrive(sz)
    part = rzs[z].astype(F32)
    for d in range(1, NZ):
        part = part + rz_in[d - 1].astype(F32)
    rng[x, z] = part.astype(BF16)
    sz = [send(rng.at[x, z], rng.at[x, z], dev(zz=zat(d))) for d in range(1, NZ)]
    arrive(sz)
    sx = [send(rng.at[x], rng.at[x], dev(xx=xat(d))) for d in range(1, NX)]
    arrive(g_h1x)
    g_h1x = h1x2()
    arrive(g_h0z)
    g_h0z = h0z(4)
    arrive(sx)

    def whole_range():
        return rng[...].reshape(w_ref.shape[0], RANK)

    def scatter_core(part_ref, core_ref):
        return [send(part_ref.at[sib], core_ref, dev(kk=sib))]

    def scatter_y(part_ref, core_ref, sum_ref, in_ref, kind):
        sum_ref[...] = (part_ref[k].astype(F32) + core_ref[...].astype(F32)).astype(kind)
        return [send(sum_ref.at[yat(d)], in_ref.at[d - 1], dev(yy=yat(d))) for d in range(1, NY)]

    def owned(sum_ref, in_ref):
        out = sum_ref[y].astype(F32)
        for d in range(1, NY):
            out = out + in_ref[d - 1].astype(F32)
        return out

    whole = whole_range()
    gp[...] = dot(whole, whole, 0, 0).reshape(gp.shape)
    s_g = scatter_core(gp, gcore)
    zp[...] = dot(whole, resid[...], 0, 0).astype(BF16).reshape(zp.shape)
    arrive(s_g)
    s_g = scatter_y(gp, gcore, gs, gy_in, F32)
    s_z = scatter_core(zp, zcore)
    for i in range(8):
        sl = slice(128 * i, 128 * i + 128)
        inv = 1.0 / scale_out[sl, 0:1]
        rscaled[sl, :] = (rng[i // 2, 4 * (i % 2):4 * (i % 2) + 4].reshape(128, RANK).astype(F32) * inv).astype(BF16)
    arrive(s_g)
    gfull[k, y] = owned(gs, gy_in)
    s_g = [send(gfull.at[k, y], gfull.at[k, y], dev(yy=yat(d))) for d in range(1, NY)]
    arrive(s_z)
    s_z = scatter_y(zp, zcore, zs, zy_in, BF16)
    arrive(s_g)
    s_g = [send(gfull.at[k], gfull.at[k], dev(kk=sib))]
    arrive(s_z)
    z_out[k, y] = owned(zs, zy_in).astype(BF16)
    s_z = [send(z_out.at[k, y], z_out.at[k, y], dev(yy=yat(d))) for d in range(1, NY)]
    arrive(g_h0z)
    arrive(g_h1x)
    arrive(s_g)

    def tokens(yy, kk):
        return cal[yy, pl.ds(kk * 4, 4)].reshape(256, w_ref.shape[0])

    for yy in range(NY):
        block = tokens(yy, sib)
        ap[sib, yy] = dot(block, rclip[...], 1, 0).astype(BF16)
        qp[sib, yy] = dot(block, rscaled[...], 1, 0).astype(BF16)
    s_a, s_q = scatter_core(ap, acore), scatter_core(qp, qcore)
    for yy in range(NY):
        block = tokens(yy, k)
        ap[k, yy] = dot(block, rclip[...], 1, 0).astype(BF16)
        qp[k, yy] = dot(block, rscaled[...], 1, 0).astype(BF16)
    arrive(s_z)
    s_z = [send(z_out.at[k], z_out.at[k], dev(kk=sib))]
    arrive(s_a)
    s_a = scatter_y(ap, acore, asum, ay_in, BF16)
    arrive(s_q)
    s_q = scatter_y(qp, qcore, qs, qy_in, BF16)

    m_ref[:, :RANK] = gfull[...].reshape(RANK, RANK)
    ii = lax.broadcasted_iota(jnp.int32, (RANK, RANK), 0)
    jj = lax.broadcasted_iota(jnp.int32, (RANK, RANK), 1)
    m_ref[:, RANK:] = jnp.where(ii == jj, 1.0, 0.0)
    inverse_factor(m_ref, linv_out)

    arrive(s_z)
    arrive(s_q)
    q_out[...] = owned(qs, qy_in)
    arrive(s_a)
    a_out[...] = owned(asum, ay_in)
    for copy in pending:
        copy.wait_send()


def output_kernel(w_ref, a_ref, q_ref, linv_ref, rng_ref, z_ref, scale_ref, tau_ref, sparse_ref, basis_ref, coeffs_ref, err_ref):
    hi, lo = split2(linv_ref[...])
    pair = jnp.concatenate([hi, lo], axis=1)
    rng = rng_ref[...]
    basis_ref[...] = dot(jnp.concatenate([rng, rng], axis=1), pair, 1, 1).astype(BF16)
    zz = z_ref[...]
    coeffs = dot(pair, jnp.concatenate([zz, zz], axis=0), 1, 0).astype(BF16)
    coeffs_ref[...] = coeffs
    qh, ql = split2(q_ref[...])
    m = dot(jnp.concatenate([qh, qh, ql], axis=1), jnp.concatenate([hi, lo, hi], axis=1), 1, 1)
    mh, ml = split2(m)
    err_ref[...] = a_ref[...] - dot(jnp.concatenate([mh, ml], axis=1), jnp.concatenate([coeffs, coeffs], axis=0), 1, 0)
    tau = tau_ref[0:1, 0:1]

    def rows(i, carry):
        sl = pl.ds(pl.multiple_of(i * 32, 32), 32)
        scaled = scale_ref[sl, 0:1] * w_ref[sl, :].astype(F32)
        sparse_ref[sl, :] = (scaled - jnp.clip(scaled, -tau, tau)).astype(BF16)
        return carry

    lax.fori_loop(0, w_ref.shape[0] // 32, rows, 0)


def shards(weight, calib, sketch):
    d, f = weight.shape
    t = calib.shape[0]
    nrow = d // NX
    vm = pltpu.VMEM
    shape = jax.ShapeDtypeStruct
    out_shape = (
        shape((256, f), F32), shape((256, RANK), F32), shape((RANK, RANK), F32), shape((NX, NZ, nrow // NZ, RANK), BF16),
        shape((2, NY, 32, f), BF16), shape((d, 128), F32), shape((8, 128), F32),
    )
    scratch = [
        vm((NX, NZ, t, d), BF16),
        vm((2, d), F32), vm((NX - 1, 2, d), F32), vm((2, d), F32), vm((NZ - 1, 2, d), F32),
        vm((8, 128), F32), vm((7, 8, 128), F32),
        vm((d, f), BF16), vm((d, f), BF16),
        vm((NX, nrow, RANK), BF16), vm((NX - 1, nrow, RANK), BF16),
        vm((NZ, nrow // NZ, RANK), BF16), vm((NZ - 1, nrow // NZ, RANK), BF16),
    ]
    for kind, n, width in ((F32, 32, RANK),):
        scratch += [vm((2, NY, n, width), kind), vm((NY, n, width), kind), vm((NY, n, width), kind), vm((NY - 1, n, width), kind)]
    scratch += [vm((8, 128), F32), vm((2, NY, 32, RANK), F32)]
    for n, width in ((32, f), (256, RANK), (256, f)):
        scratch += [vm((2, NY, n, width), BF16), vm((NY, n, width), BF16), vm((NY, n, width), BF16), vm((NY - 1, n, width), BF16)]
    scratch += [vm((RANK, 2 * RANK), F32), vm((d, RANK), BF16)]
    scratch += [pltpu.SemaphoreType.DMA((128,)), pltpu.SemaphoreType.DMA((128,))]
    whole = pl.BlockSpec(memory_space=vm)
    a, q, linv, rng, zz, scale, tau = pl.pallas_call(
        exchange_kernel,
        out_shape=out_shape,
        in_specs=[whole] * 3,
        out_specs=[whole] * len(out_shape),
        scratch_shapes=scratch,
        compiler_params=pltpu.CompilerParams(collective_id=0, has_side_effects=True, vmem_limit_bytes=60 * 2**20),
    )(weight, calib, sketch)
    return pl.pallas_call(
        output_kernel,
        out_shape=(shape((d, f), BF16), shape((d, RANK), BF16), shape((RANK, f), BF16), shape((256, f), F32)),
        in_specs=[whole] * 8,
        out_specs=[whole] * 4,
        compiler_params=pltpu.CompilerParams(vmem_limit_bytes=60 * 2**20),
    )(weight, a, q, linv, rng.reshape(d, RANK), zz.reshape(RANK, f), scale, tau)


def solution(mesh):
    return jax.shard_map(
        shards,
        mesh=mesh,
        in_specs=(P("cols", "rows"), P("rows", "cols"), P("rows", None)),
        out_specs=(P("cols", "rows"), P("cols", None), P(None, "rows"), P("cols", "rows")),
        check_vma=False,
    )
```

time: 544 us -> 121 us (0.22)
  waiting for transfers between devices: 239 us -> 0 us
  blocking collectives: 183 us -> 0 us
  Pallas kernels: 0 us -> 120 us
  other arithmetic: 66.9 us -> 0 us
  matrix products: 24.2 us -> 0 us
  between operations: 15.9 us -> 0.64 us
  local copies, waits for them, and re-layouts: 11.3 us -> 0 us
    psum x2 -> x0, waiting for transfers between devices: 204 us -> none  [the longest x1 140 us: shards(): ranged = lax.psum(partial_value, 'rows')]
    psum x3 -> x0, blocking collectives: 183 us -> none  [the longest x1 88.1 us: shards(): total = lax.psum(jnp.sum(jnp.abs(scaled)), ('rows', 'cols'))]
    pallas_call x0 -> x2, Pallas kernels: none -> 120 us  [the longest x1 112 us: shards(): pl.pallas_call(exchange_kernel, out_shape=out_shape, in_specs=[whole] * 3...]
    another operation x9 -> x0, other arithmetic: 56.8 us -> none  [the longest x6 34.6 us: orthonormal(): chol = jnp.linalg.cholesky(gram)]
    reduce_scatter x1 -> x0, waiting for transfers between devices: 35.4 us -> none  [shards(): lax.psum_scatter(jnp.dot(whole_x, err, preferred_element_type=jnp.float32...]
    dot_general x4 -> x0, matrix products: 18.2 us -> none  [the longest x1 8.91 us: shards(): jnp.dot(whole_x, err, preferred_element_type=jnp.float32)]
    another operation x9 -> x0, local copies, waits for them, and re-layouts: 7.74 us -> none
    another operation x5 -> x0, matrix products: 5.98 us -> none  [the longest x3 3.2 us: orthonormal(): jax.scipy.linalg.solve_triangular(chol, ranged.T, lower=True)]
  transfers between devices with their start and end apart: 4 -> 0, of which waited for: 3 -> 0; matrix products, arithmetic and copies ran while one was open for 15% -> 0% of each run, Pallas kernels for 0% -> 0%
where the time goes in v1:
time: 121 us
  Pallas kernels  120 us (99%)
    pallas_call x1, Pallas kernels, shards(): pl.pallas_call(exchange_kernel, out_shape=out_shape, in_specs=[whole] * 3...  112 us
    pallas_call x1, Pallas kernels, shards(): pl.pallas_call(output_kernel, out_shape=(shape((d, f), BF16), shape((d, R...  8.3 us

profile of v1, /device:TPU:1, one launch (start us, length us, event | category | flops | bytes accessed | tf_op | source)
XLA Modules:
  0.0 120.6 jit_solution(13955417349675668125)
XLA Ops:
  0.6 111.7 %shard_map.66 = (f32[256,896]{1,0:T(8,128)}, f32[256,256]{1,0:T(8,128)}, f32[256,256]{1,0:T(8,128)}, bf16[4,8,32,256]{3,2,1,0:T(8,128)(2,1)}, bf16[2,4,32,896]{3...) custom-call(bf16[1024,896]{1,0:T(8,128)(2,1)} %w_ref.3, bf16[64,1024]{1,0:T(8,128)(2,1)} %cal_in.1, ...), custom_call_target="tpu_custom_call" | custom-call | tf_op jit(solution)/shard_map/pallas_call | solution.py:364
  112.3 8.3 %shard_map.67 = (bf16[1024,896]{1,0:T(8,128)(2,1)}, bf16[1024,256]{1,0:T(8,128)(2,1)}, bf16[256,896]{1,0:T(8,128)(2,1)}, f32[256,896]{1,0:T(8,128)}) custom-call(bf16[1024,896]{1,0:T(8,128)(2,1)} %w_ref.3, f32[256,896]{1,0:T(8,128)} %get-tuple-element.11.a_ref, f32[256,256]{1,0:T(8,128)} %get-tuple-element.12.q_ref, f32[256,256]{1,0:T(8,128)} %get-tuple-element.13.linv_ref, ...), custom_call_target="tpu_custom_call" | custom-call | tf_op jit(solution)/shard_map/pallas_call | solution.py:372

commit v2 on v1

v2 whole, which is shorter than its diff:
```python
import jax
import jax.numpy as jnp
from jax import lax
from jax.experimental import pallas as pl
from jax.experimental.pallas import tpu as pltpu
from jax.sharding import PartitionSpec as P

MESH = pl.DeviceIdType.MESH
F32, BF16 = jnp.float32, jnp.bfloat16
NX, NZ, NY = 4, 8, 4
RANK = 256
PANEL = 32
CUT = 32


def split3(v):
    a = v.astype(BF16)
    rest = v - a.astype(F32)
    b = rest.astype(BF16)
    return a, b, (rest - b.astype(F32)).astype(BF16)


def split2(v):
    a = v.astype(BF16)
    return a, (v - a.astype(F32)).astype(BF16)


def dot(a, b, ca, cb):
    return lax.dot_general(a, b, (((ca,), (cb,)), ((), ())), preferred_element_type=F32)


def inverse_factor(m_ref, out_ref):
    lane = lax.broadcasted_iota(jnp.int32, (PANEL, 2 * RANK), 1)
    sub8 = lax.broadcasted_iota(jnp.int32, (8, 128), 0)
    groups = PANEL // 8

    def panel(step, carry):
        k0 = pl.multiple_of(step * PANEL, PANEL)
        rows = m_ref[pl.ds(k0, PANEL), :]
        rows = jnp.where(lane >= k0, rows, 0.0)
        diag = pltpu.roll(rows[:, :RANK], lax.rem(RANK - k0, RANK), 1)[:, :128]
        rg = [rows[8 * g:8 * g + 8, :] for g in range(groups)]
        dg = [diag[8 * g:8 * g + 8, :] for g in range(groups)]
        for q in range(groups):
            left = range(groups - q)
            col = [
                [jnp.broadcast_to(dg[g][:, 8 * q + j:8 * q + j + 1], (8, 128)) for g in range(q, groups)]
                for j in range(8)
            ]
            pivots = jnp.zeros((8, 128), F32)
            for j in range(8):
                pivot = jnp.broadcast_to(col[j][0][j:j + 1, :], (8, 128))
                inv = 1.0 / pivot
                pivots = jnp.where(sub8 == j, pivot, pivots)
                mult = [col[j][g] * inv for g in left]
                mult[0] = jnp.where(sub8 > j, mult[0], 0.0)
                for other in range(j + 1, 8):
                    row = jnp.broadcast_to(col[other][0][j:j + 1, :], (8, 128))
                    for g in left:
                        col[other][g] = col[other][g] - mult[g] * row
                rrow, drow = rg[q][j:j + 1, :], dg[q][j:j + 1, :]
                for g in left:
                    rg[q + g] = rg[q + g] - jnp.concatenate([mult[g]] * 4, axis=1) * rrow
                    dg[q + g] = dg[q + g] - mult[g] * drow
            root = lax.rsqrt(pivots)
            rg[q] = rg[q] * jnp.concatenate([root] * 4, axis=1)
        done = jnp.concatenate(rg, axis=0)
        out_ref[pl.ds(k0, PANEL), :] = done[:, RANK:]
        a, b, c = split3(done)
        lhs = jnp.concatenate([a, a, b, a, b, c], axis=0)[:, :RANK]
        rhs = jnp.concatenate([a, b, a, c, b, a], axis=0)
        m_ref[...] -= dot(lhs, rhs, 0, 0)
        return carry

    lax.fori_loop(0, RANK // PANEL, panel, 0)


def exchange_kernel(
    w_in, cal_in, sk_in,
    a_out, q_out, linv_out, rng_out, z_out, scale_out, tau_out,
    w_ref, sk_ref, cal, stx, stx_in, stz, stz_in, tsend, t_in, tau_ref, scale, resid, rclip, rp, rx_in, rzs, rz_in, rng, rscaled,
    gp, gcore, gs, gy_in, gfull, zp, zcore, zs, zy_in, zfull, qp, qcore, qs, qy_in, qsum, ap, acore, asum, ay1, ay2, atot, m_ref, linv,
    ssem, rsem, lsem,
):
    rr, cc = lax.axis_index("rows"), lax.axis_index("cols")
    x, z = rr // NZ, lax.rem(rr, NZ)
    y, k = cc // 2, lax.rem(cc, 2)
    sib = 1 - k
    rows_d, cols_f = w_ref.shape

    def xat(d):
        return lax.rem(x + d, NX)

    def zat(d):
        return lax.rem(z + d, NZ)

    def yat(d):
        return lax.rem(y + d, NY)

    def dev(xx=x, zz=z, yy=y, kk=k):
        return (xx * NZ + zz, yy * 2 + kk)

    used = [0, 0]
    pending, stores = [], []

    def send(src, dst, to):
        i = used[0]
        used[0] += 1
        copy = pltpu.make_async_remote_copy(
            src_ref=src, dst_ref=dst, send_sem=ssem.at[i], recv_sem=rsem.at[i], device_id=to, device_id_type=MESH
        )
        copy.start()
        pending.append(copy)
        return copy

    def arrive(copies):
        for copy in copies:
            copy.wait_recv()

    def local(src, dst):
        i = used[1]
        used[1] += 1
        copy = pltpu.make_async_copy(src, dst, lsem.at[i])
        copy.start()
        return copy

    def store(src, dst):
        stores.append(local(src, dst))

    load_cal = local(cal_in, cal.at[x, z])
    load_w = local(w_in, w_ref)
    load_sk = local(sk_in, sk_ref)

    barrier = pltpu.get_barrier_semaphore()
    partners = [dev(xx=xat(d)) for d in range(1, NX)] + [dev(zz=zat(d)) for d in range(1, NZ)]
    partners += [(rr, lax.rem(cc + d, 8)) for d in range(1, 8)]
    for p in partners:
        pl.semaphore_signal(barrier, inc=1, device_id=p, device_id_type=MESH)

    load_cal.wait()
    for i in range(2):
        part = cal[x, z, :, 512 * i:512 * i + 512].astype(F32)
        stx[0:1, 512 * i:512 * i + 512] = jnp.sum(part * part, axis=0, keepdims=True)
    load_w.wait()
    ones = jnp.ones((8, cols_f), BF16)
    for i in range(4):
        stx[1:2, 256 * i:256 * i + 256] = dot(ones, jnp.abs(w_ref[256 * i:256 * i + 256, :]), 1, 1)[0:1, :]
    pl.semaphore_wait(barrier, len(partners))

    xp, xm, zp_, zm = xat(1), xat(NX - 1), zat(1), zat(NZ - 1)
    half = rows_d // 2
    lower, upper = pl.ds(0, half), pl.ds(half, half)
    first, second = pl.ds(0, CUT), pl.ds(CUT, 64 - CUT)

    def both(up, down, along):
        if along == 0:
            return [send(up, up, dev(xx=xp)), send(down, down, dev(xx=xm))]
        return [send(up, up, dev(zz=zp_)), send(down, down, dev(zz=zm))]

    def lane_first():
        copies = both(cal.at[x, z, first], cal.at[x, z, first], 0)
        yield
        arrive(copies)
        copies = both(cal.at[xm, z, first, lower], cal.at[xp, z, first, upper], 0)
        yield
        arrive(copies)
        for step in range(1, 5):
            part = (slice(None),) * 2 if step < 4 else (lower, upper)
            copies = both(cal.at[:, zat(NZ - step + 1), first, part[0]], cal.at[:, zat(step - 1), first, part[1]], 1)
            yield
            arrive(copies)
        yield

    def lane_second():
        for step in range(1, 5):
            part = (slice(None),) * 2 if step < 4 else (lower, upper)
            copies = both(cal.at[x, zat(NZ - step + 1), second, part[0]], cal.at[x, zat(step - 1), second, part[1]], 1)
            yield
            arrive(copies)
        copies = both(cal.at[x, :, second], cal.at[x, :, second], 0)
        yield
        arrive(copies)
        copies = both(cal.at[xm, :, second, lower], cal.at[xp, :, second, upper], 0)
        yield
        arrive(copies)
        yield

    lane1, lane2 = lane_first(), lane_second()

    sx = [send(stx, stx_in.at[d - 1], dev(xx=xat(d))) for d in range(1, NX)]
    next(lane1)
    next(lane2)
    arrive(sx)
    stz[...] = stx[...] + stx_in[0] + stx_in[1] + stx_in[2]
    sz = [send(stz, stz_in.at[d - 1], dev(zz=zat(d))) for d in range(1, NZ)]
    next(lane1)
    next(lane2)
    arrive(sz)
    tot = stz[...]
    for d in range(1, NZ):
        tot = tot + stz_in[d - 1]
    scale_row = jnp.sqrt(tot[0:1, :] / (NX * NZ * cal_in.shape[0]) + 1e-06)
    mine = jnp.sum(scale_row * tot[1:2, :], axis=1, keepdims=True)
    tsend[...] = jnp.broadcast_to(mine, (8, 128))
    st = [send(tsend, t_in.at[d - 1], (rr, lax.rem(cc + d, 8))) for d in range(1, 8)]
    next(lane1)
    next(lane2)
    for i in range(8):
        row = scale_row[:, 128 * i:128 * i + 128]
        scale[128 * i:128 * i + 128, :] = jnp.transpose(jnp.broadcast_to(row, (128, 128)))
    store(scale, scale_out)
    arrive(st)
    total = tsend[...]
    for d in range(1, 8):
        total = total + t_in[d - 1]
    tau_ref[...] = total * (2.0 / (float(rows_d * 8) * float(cols_f * NX * NZ)))
    store(tau_ref, tau_out)
    tau = tau_ref[0:1, 0:1]

    def clip_rows(i, carry):
        sl = pl.ds(pl.multiple_of(i * 32, 32), 32)
        sc = scale[sl, 0:1]
        lim = tau / sc
        w = w_ref[sl, :].astype(F32)
        resid[sl, :] = jnp.clip(sc * w, -tau, tau).astype(BF16)
        rclip[sl, :] = jnp.clip(w, -lim, lim).astype(BF16)
        return carry

    next(lane2)
    lax.fori_loop(0, rows_d // 32, clip_rows, 0)

    nrow = rows_d // NX
    load_sk.wait()
    sx = []
    for d in (2, 1, 3, 0):
        i = xat(d)
        rp[i] = dot(resid[pl.ds(pl.multiple_of(i * nrow, nrow), nrow), :], sk_ref[...], 1, 0).astype(BF16)
        if d:
            sx.append(send(rp.at[i], rx_in.at[d - 1], dev(xx=i)))
    next(lane1)
    next(lane2)
    arrive(sx)
    part = rp[x].astype(F32)
    for d in range(1, NX):
        part = part + rx_in[d - 1].astype(F32)
    rzs[...] = part.astype(BF16).reshape(NZ, nrow // NZ, RANK)
    sz = [send(rzs.at[zat(d)], rz_in.at[d - 1], dev(zz=zat(d))) for d in range(1, NZ)]
    next(lane1)
    arrive(sz)
    part = rzs[z].astype(F32)
    for d in range(1, NZ):
        part = part + rz_in[d - 1].astype(F32)
    rng[x, z] = part.astype(BF16)
    sz = [send(rng.at[x, z], rng.at[x, z], dev(zz=zat(d))) for d in range(1, NZ)]
    next(lane1)
    next(lane2)

    def scatter_core(part_ref, core_ref):
        return [send(part_ref.at[sib], core_ref, dev(kk=sib))]

    def lane_products(b, tokens, n):
        def fill(kk):
            for yy in range(NY):
                block = cal[yy, pl.ds(kk * 4, 4), tokens].reshape(4 * n, rows_d)
                ap[b][kk, yy] = dot(block, rclip[...], 1, 0).astype(BF16)

        fill(sib)
        copies = scatter_core(ap[b], acore[b])
        fill(k)
        yield
        arrive(copies)
        for yy in range(NY):
            asum[b][yy] = (ap[b][k, yy].astype(F32) + acore[b][yy].astype(F32)).astype(BF16)
        lo, hi = pl.ds(0, 2 * n), pl.ds(2 * n, 2 * n)
        yp, ym = yat(1), yat(NY - 1)
        copies = [send(asum[b].at[yat(2), lo], ay1[b].at[0], dev(yy=yp)), send(asum[b].at[yat(2), hi], ay1[b].at[1], dev(yy=ym))]
        yield
        arrive(copies)
        asum[b][yp, lo] = (asum[b][yp, lo].astype(F32) + ay1[b][0].astype(F32)).astype(BF16)
        asum[b][ym, hi] = (asum[b][ym, hi].astype(F32) + ay1[b][1].astype(F32)).astype(BF16)
        copies = [send(asum[b].at[yp], ay2[b].at[0], dev(yy=yp)), send(asum[b].at[ym], ay2[b].at[1], dev(yy=ym))]
        yield
        arrive(copies)
        whole = asum[b][y].astype(F32) + ay2[b][0].astype(F32) + ay2[b][1].astype(F32)
        atot[:, tokens, :] = whole.reshape(4, n, cols_f)
        yield

    batch1, batch2 = lane_products(0, first, CUT), lane_products(1, second, 64 - CUT)

    arrive(sz)
    sx = [send(rng.at[x], rng.at[x], dev(xx=xat(d))) for d in range(1, NX)]
    next(lane1)
    next(batch1)
    next(batch1)
    next(lane2)
    next(batch2)
    next(batch1)
    arrive(sx)
    store(rng, rng_out)

    def scatter_y(part_ref, core_ref, sum_ref, in_ref, kind):
        sum_ref[...] = (part_ref[k].astype(F32) + core_ref[...].astype(F32)).astype(kind)
        return [send(sum_ref.at[yat(d)], in_ref.at[d - 1], dev(yy=yat(d))) for d in range(1, NY)]

    def owned(sum_ref, in_ref):
        out = sum_ref[y].astype(F32)
        for d in range(1, NY):
            out = out + in_ref[d - 1].astype(F32)
        return out

    whole = rng[...].reshape(rows_d, RANK)
    gp[...] = dot(whole, whole, 0, 0).reshape(gp.shape)
    s_g = scatter_core(gp, gcore)
    zp[...] = dot(whole, resid[...], 0, 0).astype(BF16).reshape(zp.shape)
    arrive(s_g)
    s_g = scatter_y(gp, gcore, gs, gy_in, F32)
    next(batch2)
    s_z = scatter_core(zp, zcore)
    for i in range(8):
        sl = slice(128 * i, 128 * i + 128)
        inv = 1.0 / scale[sl, 0:1]
        rscaled[sl, :] = (rng[i // 2, 4 * (i % 2):4 * (i % 2) + 4].reshape(128, RANK).astype(F32) * inv).astype(BF16)
    arrive(s_g)
    gfull[k, y] = owned(gs, gy_in)
    s_g = [send(gfull.at[k, y], gfull.at[k, y], dev(yy=yat(d))) for d in range(1, NY)]
    next(batch2)
    arrive(s_z)
    s_z = scatter_y(zp, zcore, zs, zy_in, BF16)
    for yy in range(NY):
        qp[sib, yy] = dot(cal[yy, pl.ds(sib * 4, 4)].reshape(256, rows_d), rscaled[...], 1, 0).astype(BF16)
    s_q = scatter_core(qp, qcore)
    for yy in range(NY):
        qp[k, yy] = dot(cal[yy, pl.ds(k * 4, 4)].reshape(256, rows_d), rscaled[...], 1, 0).astype(BF16)
    arrive(s_g)
    s_g = [send(gfull.at[k], gfull.at[k], dev(kk=sib))]
    arrive(s_q)
    s_q = scatter_y(qp, qcore, qs, qy_in, BF16)
    arrive(s_z)
    zfull[k, y] = owned(zs, zy_in).astype(BF16)
    s_z = [send(zfull.at[k, y], zfull.at[k, y], dev(yy=yat(d))) for d in range(1, NY)]
    arrive(s_g)

    m_ref[:, :RANK] = gfull[...].reshape(RANK, RANK)
    ii = lax.broadcasted_iota(jnp.int32, (RANK, RANK), 0)
    jj = lax.broadcasted_iota(jnp.int32, (RANK, RANK), 1)
    m_ref[:, RANK:] = jnp.where(ii == jj, 1.0, 0.0)
    inverse_factor(m_ref, linv)
    store(linv, linv_out)

    arrive(s_z)
    s_z = [send(zfull.at[k], zfull.at[k], dev(kk=sib))]
    next(batch1)
    next(batch2)
    store(atot, a_out)
    arrive(s_q)
    qsum[...] = owned(qs, qy_in)
    store(qsum, q_out)
    arrive(s_z)
    store(zfull, z_out)
    for copy in pending:
        copy.wait_send()
    for copy in stores:
        copy.wait()


def output_kernel(
    w_in, a_in, q_in, linv_in, rng_in, z_in, scale_in, tau_in, sparse_out, basis_out, coeffs_out, err_out,
    w_ref, a_ref, q_ref, linv_ref, rng_ref, z_ref, scale_ref, tau_ref, sparse_ref, basis_ref, coeffs_ref, err_ref, lsem,
):
    used = [0]

    def copy(src, dst):
        i = used[0]
        used[0] += 1
        out = pltpu.make_async_copy(src, dst, lsem.at[i])
        out.start()
        return out

    parts = 4
    n = w_ref.shape[0] // parts
    cut = [pl.ds(i * n, n) for i in range(parts)]
    small = [copy(tau_in, tau_ref), copy(scale_in, scale_ref)]
    loads_w = [copy(w_in.at[c], w_ref.at[c]) for c in cut]
    loads_b = [copy(linv_in, linv_ref), copy(rng_in, rng_ref)]
    load_z, load_q, load_a = copy(z_in, z_ref), copy(q_in, q_ref), copy(a_in, a_ref)
    for c in small:
        c.wait()
    tau = tau_ref[0:1, 0:1]
    stores = []
    for p in range(parts):
        loads_w[p].wait()

        def rows(i, carry, p=p):
            sl = pl.ds(pl.multiple_of(p * n + i * 32, 32), 32)
            scaled = scale_ref[sl, 0:1] * w_ref[sl, :].astype(F32)
            sparse_ref[sl, :] = (scaled - jnp.clip(scaled, -tau, tau)).astype(BF16)
            return carry

        lax.fori_loop(0, n // 32, rows, 0)
        stores.append(copy(sparse_ref.at[cut[p]], sparse_out.at[cut[p]]))
    for c in loads_b:
        c.wait()
    hi, lo = split2(linv_ref[...])
    pair = jnp.concatenate([hi, lo], axis=1)
    rng = rng_ref[...]
    basis_ref[...] = dot(jnp.concatenate([rng, rng], axis=1), pair, 1, 1).astype(BF16)
    stores.append(copy(basis_ref, basis_out))
    load_z.wait()
    zz = z_ref[...]
    coeffs = dot(pair, jnp.concatenate([zz, zz], axis=0), 1, 0).astype(BF16)
    coeffs_ref[...] = coeffs
    stores.append(copy(coeffs_ref, coeffs_out))
    load_q.wait()
    qh, ql = split2(q_ref[...])
    m = dot(jnp.concatenate([qh, qh, ql], axis=1), jnp.concatenate([hi, lo, hi], axis=1), 1, 1)
    mh, ml = split2(m)
    load_a.wait()
    err_ref[...] = a_ref[...] - dot(jnp.concatenate([mh, ml], axis=1), jnp.concatenate([coeffs, coeffs], axis=0), 1, 0)
    stores.append(copy(err_ref, err_out))
    for c in stores:
        c.wait()


def shards(weight, calib, sketch):
    d, f = weight.shape
    t = calib.shape[0]
    nrow = d // NX
    vm = pltpu.VMEM
    shape = jax.ShapeDtypeStruct
    out_shape = (
        shape((4, t, f), F32), shape((256, RANK), F32), shape((RANK, RANK), F32), shape((NX, NZ, nrow // NZ, RANK), BF16),
        shape((2, NY, 32, f), BF16), shape((d, 128), F32), shape((8, 128), F32),
    )

    def scatter(n, width, kind):
        return [vm((2, NY, n, width), kind), vm((NY, n, width), kind), vm((NY, n, width), kind), vm((NY - 1, n, width), kind)]

    batches = (CUT, t - CUT)
    scratch = [
        vm((d, f), BF16), vm((f, RANK), BF16), vm((NX, NZ, t, d), BF16),
        vm((2, d), F32), vm((NX - 1, 2, d), F32), vm((2, d), F32), vm((NZ - 1, 2, d), F32),
        vm((8, 128), F32), vm((7, 8, 128), F32), vm((8, 128), F32), vm((d, 128), F32),
        vm((d, f), BF16), vm((d, f), BF16),
        vm((NX, nrow, RANK), BF16), vm((NX - 1, nrow, RANK), BF16),
        vm((NZ, nrow // NZ, RANK), BF16), vm((NZ - 1, nrow // NZ, RANK), BF16),
        vm((NX, NZ, nrow // NZ, RANK), BF16), vm((d, RANK), BF16),
        *scatter(32, RANK, F32), vm((2, NY, 32, RANK), F32),
        *scatter(32, f, BF16), vm((2, NY, 32, f), BF16),
        *scatter(256, RANK, BF16), vm((256, RANK), F32),
        [vm((2, NY, 4 * n, f), BF16) for n in batches],
        [vm((NY, 4 * n, f), BF16) for n in batches],
        [vm((NY, 4 * n, f), BF16) for n in batches],
        [vm((2, 2 * n, f), BF16) for n in batches],
        [vm((2, 4 * n, f), BF16) for n in batches],
        vm((4, t, f), F32), vm((RANK, 2 * RANK), F32), vm((RANK, RANK), F32),
        pltpu.SemaphoreType.DMA((128,)), pltpu.SemaphoreType.DMA((128,)), pltpu.SemaphoreType.DMA((16,)),
    ]
    anywhere = pl.BlockSpec(memory_space=pl.ANY)
    a, q, linv, rng, zz, scale, tau = pl.pallas_call(
        exchange_kernel,
        out_shape=out_shape,
        in_specs=[anywhere] * 3,
        out_specs=[anywhere] * len(out_shape),
        scratch_shapes=scratch,
        compiler_params=pltpu.CompilerParams(collective_id=0, has_side_effects=True, vmem_limit_bytes=60 * 2**20),
    )(weight, calib, sketch)
    ins = (weight, a.reshape(256, f), q, linv, rng.reshape(d, RANK), zz.reshape(RANK, f), scale, tau)
    out_shape = (shape((d, f), BF16), shape((d, RANK), BF16), shape((RANK, f), BF16), shape((256, f), F32))
    return pl.pallas_call(
        output_kernel,
        out_shape=out_shape,
        in_specs=[anywhere] * 8,
        out_specs=[anywhere] * 4,
        scratch_shapes=[vm(v.shape, v.dtype) for v in (*ins, *out_shape)] + [pltpu.SemaphoreType.DMA((24,))],
        compiler_params=pltpu.CompilerParams(vmem_limit_bytes=60 * 2**20),
    )(*ins)


def solution(mesh):
    return jax.shard_map(
        shards,
        mesh=mesh,
        in_specs=(P("cols", "rows"), P("rows", "cols"), P("rows", None)),
        out_specs=(P("cols", "rows"), P("cols", None), P(None, "rows"), P("cols", "rows")),
        check_vma=False,
    )
```

time: 121 us -> 107 us (0.88)
  Pallas kernels: 120 us -> 106 us
    pallas_call x2, Pallas kernels: 120 us -> 106 us  [the longest x1 98.4 us: shards(): pl.pallas_call(exchange_kernel, out_shape=out_shape, in_specs=[anywhere]...]
where the time goes in v2:
time: 107 us
  Pallas kernels  106 us (99%)
    pallas_call x1, Pallas kernels, shards(): pl.pallas_call(exchange_kernel, out_shape=out_shape, in_specs=[anywhere]...  98.4 us
    pallas_call x1, Pallas kernels, shards(): pl.pallas_call(output_kernel, out_shape=out_shape, in_specs=[anywhere] *...  7.5 us

profile of v2, /device:TPU:1, one launch (start us, length us, event | category | flops | bytes accessed | tf_op | source)
XLA Modules:
  0.0 106.6 jit_solution(16098736401010854265)
XLA Ops:
  0.6 98.4 %shard_map.66 = (f32[4,64,896]{2,1,0:T(8,128)}, f32[256,256]{1,0:T(8,128)}, f32[256,256]{1,0:T(8,128)}, bf16[4,8,32,256]{3,2,1,0:T(8,128)(2,1)}, bf16[2,4,32,896...) custom-call(bf16[1024,896]{1,0:T(8,128)(2,1)} %w_in.3, bf16[64,1024]{1,0:T(8,128)(2,1)} %cal_in.1, ...), custom_call_target="tpu_custom_call" | custom-call | tf_op jit(solution)/shard_map/pallas_call | solution.py:459
  99.1 7.5 %shard_map.67 = (bf16[1024,896]{1,0:T(8,128)(2,1)}, bf16[1024,256]{1,0:T(8,128)(2,1)}, bf16[256,896]{1,0:T(8,128)(2,1)}, f32[256,896]{1,0:T(8,128)}) custom-call(bf16[1024,896]{1,0:T(8,128)(2,1)} %w_in.3, f32[256,896]{1,0:T(8,128)} %bitcast.3, f32[256,256]{1,0:T(8,128)} %get-tuple-element.12.q_in, f32[256,256]{1,0:T(8,128)} %get-tuple-element.13.linv_in, ...), custom_call_target="tpu_custom_call" | custom-call | tf_op jit(solution)/shard_map/pallas_call | solution.py:469

commit v3 on v2

--- a/solution.py
+++ b/solution.py
@@ -29,7 +29,7 @@
     return lax.dot_general(a, b, (((ca,), (cb,)), ((), ())), preferred_element_type=F32)
 
 
-def inverse_factor(m_ref, out_ref):
+def inverse_factor(m_ref, out_ref, start, stop):
     lane = lax.broadcasted_iota(jnp.int32, (PANEL, 2 * RANK), 1)
     sub8 = lax.broadcasted_iota(jnp.int32, (8, 128), 0)
     groups = PANEL // 8
@@ -72,14 +72,14 @@
         m_ref[...] -= dot(lhs, rhs, 0, 0)
         return carry
 
-    lax.fori_loop(0, RANK // PANEL, panel, 0)
+    lax.fori_loop(start, stop, panel, 0)
 
 
 def exchange_kernel(
     w_in, cal_in, sk_in,
     a_out, q_out, linv_out, rng_out, z_out, scale_out, tau_out,
     w_ref, sk_ref, cal, stx, stx_in, stz, stz_in, tsend, t_in, tau_ref, scale, resid, rclip, rp, rx_in, rzs, rz_in, rng, rscaled,
-    gp, gcore, gs, gy_in, gfull, zp, zcore, zs, zy_in, zfull, qp, qcore, qs, qy_in, qsum, ap, acore, asum, ay1, ay2, atot, m_ref, linv,
+    gp, gcore, gs, gy_in, gfull, zp, zcore, zs, zy_in, zfull, qp, qcore, qs, qy_in, qfull, ap, acore, asum, ay1, ay2, atot, m_ref, linv,
     ssem, rsem, lsem,
 ):
     rr, cc = lax.axis_index("rows"), lax.axis_index("cols")
@@ -219,15 +219,51 @@
 
     def clip_rows(i, carry):
         sl = pl.ds(pl.multiple_of(i * 32, 32), 32)
-        sc = scale[sl, 0:1]
+        sc = scale[sl, :]
         lim = tau / sc
-        w = w_ref[sl, :].astype(F32)
-        resid[sl, :] = jnp.clip(sc * w, -tau, tau).astype(BF16)
-        rclip[sl, :] = jnp.clip(w, -lim, lim).astype(BF16)
+        for t in range(cols_f // 128):
+            tl = pl.ds(128 * t, 128)
+            w = w_ref[sl, tl].astype(F32)
+            resid[sl, tl] = jnp.clip(sc * w, -tau, tau).astype(BF16)
+            rclip[sl, tl] = jnp.clip(w, -lim, lim).astype(BF16)
         return carry
 
-    next(lane2)
-    lax.fori_loop(0, rows_d // 32, clip_rows, 0)
+    lax.fori_loop(0, rows_d // 64, clip_rows, 0)
+    next(lane1)
+    next(lane2)
+    lax.fori_loop(rows_d // 64, rows_d // 32, clip_rows, 0)
+
+    def scatter_core(part_ref, core_ref):
+        return [send(part_ref.at[sib], core_ref, dev(kk=sib))]
+
+    def lane_products(b, tokens, n):
+        def fill(kk):
+            for yy in range(NY):
+                block = cal[yy, pl.ds(kk * 4, 4), tokens].reshape(4 * n, rows_d)
+                ap[b][kk, yy] = dot(block, rclip[...], 1, 0).astype(BF16)
+
+        fill(sib)
+        copies = scatter_core(ap[b], acore[b])
+        fill(k)
+        yield
+        arrive(copies)
+        for yy in range(NY):
+            asum[b][yy] = (ap[b][k, yy].astype(F32) + acore[b][yy].astype(F32)).astype(BF16)
+        lo, hi = pl.ds(0, 2 * n), pl.ds(2 * n, 2 * n)
+        yp, ym = yat(1), yat(NY - 1)
+        copies = [send(asum[b].at[yat(2), lo], ay1[b].at[0], dev(yy=yp)), send(asum[b].at[yat(2), hi], ay1[b].at[1], dev(yy=ym))]
+        yield
+        arrive(copies)
+        asum[b][yp, lo] = (asum[b][yp, lo].astype(F32) + ay1[b][0].astype(F32)).astype(BF16)
+        asum[b][ym, hi] = (asum[b][ym, hi].astype(F32) + ay1[b][1].astype(F32)).astype(BF16)
+        copies = [send(asum[b].at[yp], ay2[b].at[0], dev(yy=yp)), send(asum[b].at[ym], ay2[b].at[1], dev(yy=ym))]
+        yield
+        arrive(copies)
+        whole = asum[b][y].astype(F32) + ay2[b][0].astype(F32) + ay2[b][1].astype(F32)
+        atot[:, tokens, :] = whole.reshape(4, n, cols_f)
+        yield
+
+    batch1, batch2 = lane_products(0, first, CUT), lane_products(1, second, 64 - CUT)
 
     nrow = rows_d // NX
     load_sk.wait()
@@ -254,47 +290,15 @@
     sz = [send(rng.at[x, z], rng.at[x, z], dev(zz=zat(d))) for d in range(1, NZ)]
     next(lane1)
     next(lane2)
-
-    def scatter_core(part_ref, core_ref):
-        return [send(part_ref.at[sib], core_ref, dev(kk=sib))]
-
-    def lane_products(b, tokens, n):
-        def fill(kk):
-            for yy in range(NY):
-                block = cal[yy, pl.ds(kk * 4, 4), tokens].reshape(4 * n, rows_d)
-                ap[b][kk, yy] = dot(block, rclip[...], 1, 0).astype(BF16)
-
-        fill(sib)
-        copies = scatter_core(ap[b], acore[b])
-        fill(k)
-        yield
-        arrive(copies)
-        for yy in range(NY):
-            asum[b][yy] = (ap[b][k, yy].astype(F32) + acore[b][yy].astype(F32)).astype(BF16)
-        lo, hi = pl.ds(0, 2 * n), pl.ds(2 * n, 2 * n)
-        yp, ym = yat(1), yat(NY - 1)
-        copies = [send(asum[b].at[yat(2), lo], ay1[b].at[0], dev(yy=yp)), send(asum[b].at[yat(2), hi], ay1[b].at[1], dev(yy=ym))]
-        yield
-        arrive(copies)
-        asum[b][yp, lo] = (asum[b][yp, lo].astype(F32) + ay1[b][0].astype(F32)).astype(BF16)
-        asum[b][ym, hi] = (asum[b][ym, hi].astype(F32) + ay1[b][1].astype(F32)).astype(BF16)
-        copies = [send(asum[b].at[yp], ay2[b].at[0], dev(yy=yp)), send(asum[b].at[ym], ay2[b].at[1], dev(yy=ym))]
-        yield
-        arrive(copies)
-        whole = asum[b][y].astype(F32) + ay2[b][0].astype(F32) + ay2[b][1].astype(F32)
-        atot[:, tokens, :] = whole.reshape(4, n, cols_f)
-        yield
-
-    batch1, batch2 = lane_products(0, first, CUT), lane_products(1, second, 64 - CUT)
+    next(batch1)
 
     arrive(sz)
     sx = [send(rng.at[x], rng.at[x], dev(xx=xat(d))) for d in range(1, NX)]
-    next(lane1)
-    next(batch1)
     next(batch1)
     next(lane2)
     next(batch2)
     next(batch1)
+    next(batch2)
     arrive(sx)
     store(rng, rng_out)
 
@@ -314,7 +318,6 @@
     zp[...] = dot(whole, resid[...], 0, 0).astype(BF16).reshape(zp.shape)
     arrive(s_g)
     s_g = scatter_y(gp, gcore, gs, gy_in, F32)
-    next(batch2)
     s_z = scatter_core(zp, zcore)
     for i in range(8):
         sl = slice(128 * i, 128 * i + 128)
@@ -327,34 +330,38 @@
     arrive(s_z)
     s_z = scatter_y(zp, zcore, zs, zy_in, BF16)
     for yy in range(NY):
-        qp[sib, yy] = dot(cal[yy, pl.ds(sib * 4, 4)].reshape(256, rows_d), rscaled[...], 1, 0).astype(BF16)
+        qp[sib, yy] = dot(cal[yy, sib * 4 + x], rscaled[...], 1, 0).astype(BF16)
     s_q = scatter_core(qp, qcore)
     for yy in range(NY):
-        qp[k, yy] = dot(cal[yy, pl.ds(k * 4, 4)].reshape(256, rows_d), rscaled[...], 1, 0).astype(BF16)
+        qp[k, yy] = dot(cal[yy, k * 4 + x], rscaled[...], 1, 0).astype(BF16)
     arrive(s_g)
     s_g = [send(gfull.at[k], gfull.at[k], dev(kk=sib))]
     arrive(s_q)
     s_q = scatter_y(qp, qcore, qs, qy_in, BF16)
-    arrive(s_z)
-    zfull[k, y] = owned(zs, zy_in).astype(BF16)
-    s_z = [send(zfull.at[k, y], zfull.at[k, y], dev(yy=yat(d))) for d in range(1, NY)]
     arrive(s_g)
 
     m_ref[:, :RANK] = gfull[...].reshape(RANK, RANK)
     ii = lax.broadcasted_iota(jnp.int32, (RANK, RANK), 0)
     jj = lax.broadcasted_iota(jnp.int32, (RANK, RANK), 1)
     m_ref[:, RANK:] = jnp.where(ii == jj, 1.0, 0.0)
-    inverse_factor(m_ref, linv)
-    store(linv, linv_out)
-
+    inverse_factor(m_ref, linv, 0, 2)
+    arrive(s_z)
+    zfull[k, y] = owned(zs, zy_in).astype(BF16)
+    s_z = [send(zfull.at[k, y], zfull.at[k, y], dev(yy=yat(d))) for d in range(1, NY)]
+    arrive(s_q)
+    qfull[x] = owned(qs, qy_in)
+    s_q = [send(qfull.at[x], qfull.at[x], dev(xx=xat(d))) for d in range(1, NX)]
+    next(batch1)
+    inverse_factor(m_ref, linv, 2, 5)
     arrive(s_z)
     s_z = [send(zfull.at[k], zfull.at[k], dev(kk=sib))]
-    next(batch1)
     next(batch2)
+    inverse_factor(m_ref, linv, 5, 8)
+    store(linv, linv_out)
+
     store(atot, a_out)
     arrive(s_q)
-    qsum[...] = owned(qs, qy_in)
-    store(qsum, q_out)
+    store(qfull, q_out)
     arrive(s_z)
     store(zfull, z_out)
     for copy in pending:
@@ -392,8 +399,11 @@
 
         def rows(i, carry, p=p):
             sl = pl.ds(pl.multiple_of(p * n + i * 32, 32), 32)
-            scaled = scale_ref[sl, 0:1] * w_ref[sl, :].astype(F32)
-            sparse_ref[sl, :] = (scaled - jnp.clip(scaled, -tau, tau)).astype(BF16)
+            sc = scale_ref[sl, :]
+            for t in range(w_ref.shape[1] // 128):
+                tl = pl.ds(128 * t, 128)
+                scaled = sc * w_ref[sl, tl].astype(F32)
+                sparse_ref[sl, tl] = (scaled - jnp.clip(scaled, -tau, tau)).astype(BF16)
             return carry
 
         lax.fori_loop(0, n // 32, rows, 0)
@@ -428,7 +438,7 @@
     vm = pltpu.VMEM
     shape = jax.ShapeDtypeStruct
     out_shape = (
-        shape((4, t, f), F32), shape((256, RANK), F32), shape((RANK, RANK), F32), shape((NX, NZ, nrow // NZ, RANK), BF16),
+        shape((4, t, f), F32), shape((NX, t, RANK), F32), shape((RANK, RANK), F32), shape((NX, NZ, nrow // NZ, RANK), BF16),
         shape((2, NY, 32, f), BF16), shape((d, 128), F32), shape((8, 128), F32),
     )
 
@@ -446,7 +456,7 @@
         vm((NX, NZ, nrow // NZ, RANK), BF16), vm((d, RANK), BF16),
         *scatter(32, RANK, F32), vm((2, NY, 32, RANK), F32),
         *scatter(32, f, BF16), vm((2, NY, 32, f), BF16),
-        *scatter(256, RANK, BF16), vm((256, RANK), F32),
+        *scatter(t, RANK, BF16), vm((NX, t, RANK), F32),
         [vm((2, NY, 4 * n, f), BF16) for n in batches],
         [vm((NY, 4 * n, f), BF16) for n in batches],
         [vm((NY, 4 * n, f), BF16) for n in batches],
@@ -464,7 +474,7 @@
         scratch_shapes=scratch,
         compiler_params=pltpu.CompilerParams(collective_id=0, has_side_effects=True, vmem_limit_bytes=60 * 2**20),
     )(weight, calib, sketch)
-    ins = (weight, a.reshape(256, f), q, linv, rng.reshape(d, RANK), zz.reshape(RANK, f), scale, tau)
+    ins = (weight, a.reshape(NX * t, f), q.reshape(NX * t, RANK), linv, rng.reshape(d, RANK), zz.reshape(RANK, f), scale, tau)
     out_shape = (shape((d, f), BF16), shape((d, RANK), BF16), shape((RANK, f), BF16), shape((256, f), F32))
     return pl.pallas_call(
         output_kernel,

time: 107 us -> 94.9 us (0.89); the launches traced: 107 us -> 93.3 us
  Pallas kernels: 106 us -> 92.7 us
    pallas_call x1, Pallas kernels: 98.4 us -> 86.8 us  [shards(): pl.pallas_call(exchange_kernel, out_shape=out_shape, in_specs=[anywhere]...]
    pallas_call x1, Pallas kernels: 7.5 us -> 5.83 us  [shards(): pl.pallas_call(output_kernel, out_shape=out_shape, in_specs=[anywhere] *...]
where the time goes in v3:
time: 94.9 us; the launch traced here: 93.3 us
  Pallas kernels  92.7 us (98%)
    pallas_call x1, Pallas kernels, shards(): pl.pallas_call(exchange_kernel, out_shape=out_shape, in_specs=[anywhere]...  86.8 us
    pallas_call x1, Pallas kernels, shards(): pl.pallas_call(output_kernel, out_shape=out_shape, in_specs=[anywhere] *...  5.83 us

profile of v3, /device:TPU:1, one launch (start us, length us, event | category | flops | bytes accessed | tf_op | source)
XLA Modules:
  0.0 93.3 jit_solution(15679459084182547929)
XLA Ops:
  0.6 86.8 %shard_map.66 = (f32[4,64,896]{2,1,0:T(8,128)}, f32[4,64,256]{2,1,0:T(8,128)}, f32[256,256]{1,0:T(8,128)}, bf16[4,8,32,256]{3,2,1,0:T(8,128)(2,1)}, bf16[2,4,32,...) custom-call(bf16[1024,896]{1,0:T(8,128)(2,1)} %w_in.3, bf16[64,1024]{1,0:T(8,128)(2,1)} %cal_in.1, ...), custom_call_target="tpu_custom_call" | custom-call | tf_op jit(solution)/shard_map/pallas_call | solution.py:469
  87.5 5.8 %shard_map.67 = (bf16[1024,896]{1,0:T(8,128)(2,1)}, bf16[1024,256]{1,0:T(8,128)(2,1)}, bf16[256,896]{1,0:T(8,128)(2,1)}, f32[256,896]{1,0:T(8,128)}) custom-call(bf16[1024,896]{1,0:T(8,128)(2,1)} %w_in.3, f32[256,896]{1,0:T(8,128)} %bitcast.4, f32[256,256]{1,0:T(8,128)} %bitcast.7, f32[256,256]{1,0:T(8,128)} %get-tuple-element.13.linv_in, ...), custom_call_target="tpu_custom_call" | custom-call | tf_op jit(solution)/shard_map/pallas_call | solution.py:479

commit v4 on v3

--- a/solution.py
+++ b/solution.py
@@ -321,8 +321,9 @@
     s_z = scatter_core(zp, zcore)
     for i in range(8):
         sl = slice(128 * i, 128 * i + 128)
-        inv = 1.0 / scale[sl, 0:1]
-        rscaled[sl, :] = (rng[i // 2, 4 * (i % 2):4 * (i % 2) + 4].reshape(128, RANK).astype(F32) * inv).astype(BF16)
+        inv = 1.0 / scale[sl, :]
+        piece = rng[i // 2, 4 * (i % 2):4 * (i % 2) + 4].reshape(128, RANK).astype(F32)
+        rscaled[sl, :] = (piece * jnp.concatenate([inv, inv], axis=1)).astype(BF16)
     arrive(s_g)
     gfull[k, y] = owned(gs, gy_in)
     s_g = [send(gfull.at[k, y], gfull.at[k, y], dev(yy=yat(d))) for d in range(1, NY)]
@@ -351,19 +352,19 @@
     arrive(s_q)
     qfull[x] = owned(qs, qy_in)
     s_q = [send(qfull.at[x], qfull.at[x], dev(xx=xat(d))) for d in range(1, NX)]
+    inverse_factor(m_ref, linv, 2, 5)
     next(batch1)
-    inverse_factor(m_ref, linv, 2, 5)
     arrive(s_z)
     s_z = [send(zfull.at[k], zfull.at[k], dev(kk=sib))]
-    next(batch2)
     inverse_factor(m_ref, linv, 5, 8)
     store(linv, linv_out)
 
-    store(atot, a_out)
     arrive(s_q)
     store(qfull, q_out)
     arrive(s_z)
     store(zfull, z_out)
+    next(batch2)
+    store(atot, a_out)
     for copy in pending:
         copy.wait_send()
     for copy in stores:

time: 94.9 us -> 95 us (level)
  no operation moved by 1% of the time
where the time goes in v4:
time: 95 us; the launch traced here: 93.6 us
  Pallas kernels  93 us (98%)
    pallas_call x1, Pallas kernels, shards(): pl.pallas_call(exchange_kernel, out_shape=out_shape, in_specs=[anywhere]...  87.1 us
    pallas_call x1, Pallas kernels, shards(): pl.pallas_call(output_kernel, out_shape=out_shape, in_specs=[anywhere] *...  5.83 us

profile of v4, /device:TPU:1, one launch (start us, length us, event | category | flops | bytes accessed | tf_op | source)
XLA Modules:
  0.0 93.6 jit_solution(5968735332616416399)
XLA Ops:
  0.6 87.1 %shard_map.66 = (f32[4,64,896]{2,1,0:T(8,128)}, f32[4,64,256]{2,1,0:T(8,128)}, f32[256,256]{1,0:T(8,128)}, bf16[4,8,32,256]{3,2,1,0:T(8,128)(2,1)}, bf16[2,4,32,...) custom-call(bf16[1024,896]{1,0:T(8,128)(2,1)} %w_in.3, bf16[64,1024]{1,0:T(8,128)(2,1)} %cal_in.1, ...), custom_call_target="tpu_custom_call" | custom-call | tf_op jit(solution)/shard_map/pallas_call | solution.py:470
  87.8 5.8 %shard_map.67 = (bf16[1024,896]{1,0:T(8,128)(2,1)}, bf16[1024,256]{1,0:T(8,128)(2,1)}, bf16[256,896]{1,0:T(8,128)(2,1)}, f32[256,896]{1,0:T(8,128)}) custom-call(bf16[1024,896]{1,0:T(8,128)(2,1)} %w_in.3, f32[256,896]{1,0:T(8,128)} %bitcast.4, f32[256,256]{1,0:T(8,128)} %bitcast.7, f32[256,256]{1,0:T(8,128)} %get-tuple-element.13.linv_in, ...), custom_call_target="tpu_custom_call" | custom-call | tf_op jit(solution)/shard_map/pallas_call | solution.py:480
